TPU v7x, 32 devices: a whole 2x2x4 slice. The times are simulated.
32 devices in a mesh: space: 16 (over z, x, core), event: 2 (over y).
Axes of the slice: x: 2, y: 2, z: 4, core: 2. Of those that a mesh axis runs over, the one named last changes fastest.
Arguments:
- green: bfloat16 [8, 512, 2, 6, 2048], P(None, 'event', None, None, 'space'), may hold values from -6 to 6
- strain: bfloat16 [48, 8, 2, 6, 2048], P('event', None, None, None, 'space'), may hold values from -6 to 6
- perturb: float32 [2048], P('space'), may hold values from -6 to 6
- pairs: int32 [48, 512], P(None, 'event'), may hold values 0 or 1
Outputs:
- hessian: float32 [2048], P(('space', 'event'))
All inputs are finite; a program needn't handle non-finite values. No bound on the sum of `pairs` on one device may be relied on, other than what follows from the above.
Results may differ from a plain program's by a relative error of at most 0.00096.
Values may be sent and summed in bfloat16 or wider, within the bound.
A program may use at most 64 MiB of HBM per device.

v0:
```python
import math

import jax
import jax.numpy as jnp
from jax import lax
from jax.sharding import PartitionSpec as P


def body(green, strain, perturb, pairs):
    freqs = green.shape[0]
    recv_dev = green.shape[1]
    comps = green.shape[3]
    cells = green.shape[4]
    n_space = lax.axis_size("space")
    n_event = lax.axis_size("event")
    everything = lax.all_gather(strain, "event", axis=0, tiled=True)
    events = everything.shape[0]
    scale_one = 1.0 / math.sqrt(12.0 * cells * n_space)
    scale_two = 1.0 / math.sqrt(12.0 * events * freqs * recv_dev * n_event)
    weighted = (everything.astype(jnp.float32) * perturb).astype(jnp.bfloat16)
    w_real = weighted[:, :, 0].reshape(events, freqs, -1)
    w_imag = weighted[:, :, 1].reshape(events, freqs, -1)
    combo = jnp.stack([jnp.stack([w_real, -w_imag], 2), jnp.stack([w_imag, w_real], 2)], 1)
    flat_green = green.reshape(freqs, recv_dev, 2, -1)
    partial_data = jnp.einsum(
        "frpk,eqfpk->fqer", flat_green, combo, preferred_element_type=jnp.float32
    )
    mask = pairs.astype(jnp.float32)
    total = lax.psum(partial_data, "space")
    resid = (scale_one * total * mask).astype(jnp.bfloat16)
    back_in = jnp.stack(
        [jnp.stack([resid[:, 0], resid[:, 1]], 2), jnp.stack([resid[:, 1], -resid[:, 0]], 2)], 1
    )
    back = jnp.einsum("fqepr,frpk->fqek", back_in, flat_green, preferred_element_type=jnp.float32)
    flat_strain = everything.reshape(events, freqs, 2, -1).astype(jnp.float32)
    terms = jnp.einsum("fqek,efqk->k", back, flat_strain)
    local_cells = terms.reshape(comps, cells).sum(0)
    summed = lax.psum_scatter(local_cells, "event", scatter_dimension=0, tiled=True)
    return scale_two * summed


def solution(mesh):
    in_specs = (
        P(None, "event", None, None, "space"),
        P("event", None, None, None, "space"),
        P("space"),
        P(None, "event"),
    )
    out_specs = P(("space", "event"))
    return jax.shard_map(body, mesh=mesh, in_specs=in_specs, out_specs=out_specs, check_vma=False)
```

profile of v0, /device:TPU:0, one launch (start us, length us, event | category | flops | bytes accessed | tf_op | source)
XLA Modules:
  0.0 153.0 jit_solution(7822767097175497985)
XLA Ops:
  6.5 0.0 all-gather.2.cloned.1.call-start
  6.5 2.0 %copy.37 = bf16[24,8,2,6,128]{4,1,3,2,0:T(8,128)(2,1)} copy(bf16[24,8,2,6,128]{4,2,3,1,0:T(2,128)(2,1)} %param.5) | data formatting | bytes 1179648 | tf_op args[1]
  8.5 0.0 all-gather.2.cloned.1.call-update
  8.5 0.0 copy-start.3
  8.5 0.0 all-reduce.3.cloned.1.call-start
  8.6 16.1 %copy.42 = bf16[8,256,2,6,128]{1,4,3,2,0:T(8,128)(2,1)} copy(bf16[8,256,2,6,128]{4,2,3,1,0:T(2,128)(2,1)} %param.4) | data formatting | bytes 12582912 | tf_op args[0]
  24.7 9.7 %all-gather.2.cloned.1.call-done = bf16[48,8,2,6,128]{4,1,3,2,0:T(8,128)(2,1)} async-done(((bf16[24,8,2,6,128]{4,1,3,2,0:T(8,128)(2,1)}), bf16[48,8,2,6,128]{4,1,3,2,0:T(8,128)(2,1)}) %all-gather.2.cloned.1.call-update) | async-done | bytes 1179664 | tf_op jit(solution)/shard_map/all_gather | solution.py:16
  34.4 0.0 copy-done.3
  34.4 1.5 multiply_convert_fusion
  35.9 0.1 slice_bitcast_fusion
  36.0 0.0 copy-start
  36.0 0.1 copy_negate_fusion
  36.1 0.1 copy.39
  36.3 0.2 maximum_bitcast_fusion
  36.4 2.4 %copy-done = bf16[8,256,2,6,128]{1,4,3,2,0:T(8,128)(2,1)S(1)} copy-done((bf16[8,256,2,6,128]{1,4,3,2,0:T(8,128)(2,1)S(1)}, bf16[8,256,2,6,128]{1,4,3,2,0:T(8,128)(2,1)}, u32[]{:S(2)}) %copy-start) | copy-done | bytes 6291480
  38.8 0.0 copy-start.4
  38.8 0.0 copy-start.2
  38.8 2.0 %fusion.4 = f32[8,2,48,256]{3,2,1,0:T(8,128)} fusion(bf16[8,256,2,768,1]{1,3,2,4,0:T(8,128)(2,1)S(1)} %bitcast.46, bf16[48,1,8,2,768]{4,0,3,1,2:T(8,128)(2,1)S(1)} %get-tuple-element.8, bf16[48,1,8,2,768]{4,0,3,1,2:T(8,128)(2,1)S(1)} %get-tuple-element.7), kind=kOutput, calls=%fused_computation.7 | convolution fusion | flops 605159424 | bytes 9437184 | tf_op jit(solution)/shard_map/frpk,eqfpk->fqer/dot_general | solution.py:25
  40.8 0.0 all-reduce.3.cloned.1.call-update
  40.9 0.0 copy-done.4
  40.9 0.6 dynamic-slice
  42.1 0.0 copy-done.2
  42.1 90.9 %all-reduce.3.cloned.1.call-done = f32[8,2,48,256]{3,2,1,0:T(8,128)} async-done(((f32[8,2,48,256]{3,2,1,0:T(8,128)}), f32[8,2,48,256]{3,2,1,0:T(8,128)}) %all-reduce.3.cloned.1.call-update) | async-done | bytes 786448 | tf_op jit(solution)/shard_map/psum | solution.py:29
  133.1 1.2 multiply_convert_fusion.1
  134.3 0.1 maximum_bitcast_fusion.2
  134.4 0.0 copy-start.1
  134.4 4.9 %convolution_bitcast_fusion = f32[768,48,8,2]{0,1,3,2:T(8,128)S(1)} fusion(bf16[8,256,2,768,1]{1,3,2,4,0:T(8,128)(2,1)} %bitcast.45, bf16[8,1,48,2,256]{4,2,0,3,1:T(8,128)(2,1)S(1)} %get-tuple-element.14, bf16[8,1,48,2,256]{4,2,0,3,1:T(8,128)(2,1)S(1)} %get-tuple-element.13), kind=kOutput, calls=%fused_computation.6 | convolution fusion | flops 604372992 | bytes 9437184 | tf_op jit(solution)/shard_map/fqepr,frpk->fqek/dot_general | solution.py:34
  139.3 0.0 copy-done.1
  139.3 1.3 multiply_reduce_fusion
  140.6 4.9 %all-reduce = f32[128]{0:T(128)S(1)} all-reduce(f32[128]{0:T(128)S(1)} %bitcast_reduce_fusion), channel_id=2, replica_groups=mesh['space'=16,'event'=2] {'event'}, use_global_device_ids=true, to_apply=%region_2.0.clone | all-reduce | flops 128 | bytes 1024
  145.6 0.6 dynamic-slice_multiply_fusion
  (4 shorter events, 0.1 us)
Async XLA Ops:
  6.5 27.9 %all-gather.2.cloned.1.call-start = ((), (), s32[]{:S(2)}) async-start(), calls=%async_computation | async-start | bytes 1769472 | tf_op jit(solution)/shard_map/all_gather | solution.py:16
  8.5 25.9 %copy-start.3 = (f32[128]{0:T(128)S(1)}, f32[128]{0:T(128)}, u32[]{:S(2)}) copy-start(f32[128]{0:T(128)} %param.6) | copy-start | bytes 1540
  8.5 124.5 %all-reduce.3.cloned.1.call-start = ((), (), s32[]{:S(2)}) async-start(), calls=%async_computation.1 | async-start | bytes 1572864 | tf_op jit(solution)/shard_map/psum | solution.py:29
  36.0 2.8 %copy-start = (bf16[8,256,2,6,128]{1,4,3,2,0:T(8,128)(2,1)S(1)}, bf16[8,256,2,6,128]{1,4,3,2,0:T(8,128)(2,1)}, u32[]{:S(2)}) copy-start(bf16[8,256,2,6,128]{1,4,3,2,0:T(8,128)(2,1)} %copy.42) | copy-start | bytes 18874372
  38.8 2.1 %copy-start.4 = (u32[32]{0:T(128)S(1)}, u32[32]{0:T(128)}, u32[]{:S(2)}) copy-start(u32[32]{0:T(128)} %constant.9) | copy-start | bytes 388
  38.8 3.3 %copy-start.2 = (s32[48,256]{1,0:T(8,128)S(1)}, s32[48,256]{1,0:T(8,128)}, u32[]{:S(2)}) copy-start(s32[48,256]{1,0:T(8,128)} %param.7) | copy-start | bytes 147460
  134.4 4.9 %copy-start.1 = (bf16[48,8,2,6,128]{4,1,3,2,0:T(8,128)(2,1)S(1)}, bf16[48,8,2,6,128]{4,1,3,2,0:T(8,128)(2,1)}, u32[]{:S(2)}) copy-start(bf16[48,8,2,6,128]{4,1,3,2,0:T(8,128)(2,1)} %all-gather.2.cloned.1.call-done) | copy-start | bytes 3538948
Sparse Core Ops, SparseCore 0:
  8.9 25.4 all-gather.1
  41.0 92.0 all-reduce.2
where the time goes:
time: 154 us; the launch traced here: 153 us
  waiting for transfers between devices  101 us (66%)
  local copies, waits for them, and re-layouts  21.2 us (14%)
  between operations  14.2 us (9%)
  matrix products  6.93 us (4%)
  other arithmetic  4.99 us (3%)
  blocking collectives  4.94 us (3%)
    psum x1, waiting for transfers between devices, body(): total = lax.psum(partial_data, 'space')  90.9 us
    unnamed x13, local copies, waits for them, and re-layouts  21 us
    all_gather x1, waiting for transfers between devices, body(): everything = lax.all_gather(strain, 'event', axis=0, tiled=True)  9.72 us
    unnamed x1, blocking collectives  4.94 us
    dot_general x1, matrix products, body(): jnp.einsum('fqepr,frpk->fqek', back_in, flat_green, preferred_element_typ...  4.89 us
  transfers between devices with their start and end apart: 2, of which 2 were waited for; matrix products, arithmetic and copies ran while one was open for 11% of the time, Pallas kernels for 0%

commit v1 on v0

v1 whole, which is shorter than its diff:
```python
import functools
import math

import jax
import jax.numpy as jnp
from jax import lax
from jax.experimental import pallas as pl
from jax.experimental.pallas import tpu as pltpu
from jax.sharding import PartitionSpec as P

MESH = pl.DeviceIdType.MESH
F32 = jnp.float32
BF16 = jnp.bfloat16


def kernel(
    n_space, n_event, inner, freqs, recv, comps, cells, events,
    green_ref, strain_ref, perturb_ref, pairs_ref, out_ref,
    raw_green, raw_strain, wide_green, wide_strain, g, s, part, got1, half, got2, res, acc, ends,
    load_sem, strain_s, strain_r, rs1_s, rs1_r, rs2_s, rs2_r, ag2_s, ag2_r, ag1_s, ag1_r, end_s, end_r,
):
    outer = n_space // inner
    tiles = recv // 128
    per_inner = freqs * tiles // inner
    per_part = freqs // inner
    rows = 2 * comps
    scale_one = 1.0 / math.sqrt(12.0 * cells * n_space)
    scale_two = 1.0 / math.sqrt(12.0 * events * n_event * freqs * recv * n_event)

    me = lax.axis_index("space")
    y = lax.axis_index("event")
    i = lax.rem(me, inner)
    o = lax.div(me, inner)

    def at_event(d):
        return {"event": lax.rem(y + d + n_event, n_event)}

    def at_inner(d):
        return {"space": o * inner + lax.rem(i + d + inner, inner)}

    def at_outer(d):
        return {"space": lax.rem(o + d + outer, outer) * inner + i}

    def remote(src, dst, send, recv_, device):
        return pltpu.make_async_remote_copy(
            src_ref=src, dst_ref=dst, send_sem=send, recv_sem=recv_, device_id=device, device_id_type=MESH
        )

    def when(cond, fn):
        if per_inner == outer:
            fn()
        else:
            pl.when(cond)(fn)

    strain_load = pltpu.make_async_copy(strain_ref, raw_strain, load_sem.at[freqs])
    strain_load.start()

    def order(k):
        return lax.rem((i + 1) * per_part + k, freqs)

    def green_load(f):
        return pltpu.make_async_copy(green_ref.at[f], raw_green.at[f], load_sem.at[f])

    for k in range(freqs):
        green_load(order(k)).start()

    barrier = pltpu.get_barrier_semaphore()
    for d in range(1, n_event):
        pl.semaphore_signal(barrier, inc=1, device_id=at_event(d), device_id_type=MESH)
    for d in range(1, inner):
        pl.semaphore_signal(barrier, inc=1, device_id=at_inner(d), device_id_type=MESH)
    for d in range(1, outer):
        pl.semaphore_signal(barrier, inc=1, device_id=at_outer(d), device_id_type=MESH)

    strain_load.wait()
    wide_strain[...] = raw_strain[...].astype(F32)
    pl.semaphore_wait(barrier, n_event + inner + outer - 3)

    def strain_copy(j, f):
        return remote(s.at[0, f], s.at[j, f], strain_s.at[j - 1, f], strain_r.at[j - 1, f], at_event(-j))

    def arrange_strain(k, carry):
        f = order(k)
        for c in range(comps):
            pieces = [
                wide_strain[pl.ds(f * rows + 2 * c + q, events, stride=freqs * rows), :] for q in range(2)
            ]
            s[0, f, :, c * cells:(c + 1) * cells] = jnp.concatenate(pieces, 0).astype(BF16)
        for j in range(1, n_event):
            strain_copy(j, f).start()
        return carry

    lax.fori_loop(0, freqs, arrange_strain, None)

    perturb = jnp.concatenate([perturb_ref[...]] * comps, 1)

    def forward(j, k, arrange):
        def one(n, carry):
            f = order(k * per_part + n)
            if arrange:
                green_load(f).wait()
                wide_green[...] = raw_green[f].astype(F32)
                for c in range(comps):
                    for p in range(2):
                        g[f, p * recv:(p + 1) * recv, c * cells:(c + 1) * cells] = wide_green[
                            pl.ds(2 * c + p, recv, stride=rows), :
                        ].astype(BF16)
            if j > 0:
                for step in range(j, j + 1):
                    strain_copy(step, f).wait_recv()
            weighted = (s[j, f].astype(F32) * perturb).astype(BF16)
            both = lax.dot_general(weighted, g[f], (((1,), (1,)), ((), ())), preferred_element_type=F32)
            real = both[:events, :recv] - both[events:, recv:]
            imag = both[events:, :recv] + both[:events, recv:]
            data = jnp.concatenate([real, imag], 0).astype(BF16)
            for t in range(tiles):
                part[j, f * tiles + t] = data[:, t * 128:(t + 1) * 128]
            return carry

        lax.fori_loop(0, per_part, one, None)
        if k < inner - 1:
            rs1_copy(j, k + 1).start()

    def rs1_copy(j, d):
        target = lax.rem(i + d, inner)
        return remote(
            part.at[j, pl.ds(target * per_inner, per_inner)], got1.at[j, d - 1],
            rs1_s.at[j, d - 1], rs1_r.at[j, d - 1], at_inner(d),
        )

    def rs2_copy(j, d):
        target = lax.rem(o + d, outer)
        return remote(half.at[j, target], got2.at[j, d - 1], rs2_s.at[j, d - 1], rs2_r.at[j, d - 1], at_outer(d))

    def rs2_sends(d):
        return lax.rem(o + d, outer) < per_inner

    def ag2_copy(j, d, t):
        spot = res.at[j, i * per_inner + t]
        return remote(spot, spot, ag2_s.at[j, d - 1], ag2_r.at[j, d - 1], at_outer(d))

    def ag1_copy(j, d, which):
        spot = res.at[j, pl.ds(which * per_inner, per_inner)]
        return remote(spot, spot, ag1_s.at[j, d - 1], ag1_r.at[j, d - 1], at_inner(d))

    def stage1(j):
        for d in range(1, inner):
            rs1_copy(j, d).wait_recv()
        for t in range(per_inner):
            total = part[j, i * per_inner + t].astype(F32)
            for d in range(1, inner):
                total += got1[j, d - 1, t].astype(F32)
            half[j, t] = total.astype(BF16)
        for d in range(1, outer):
            when(rs2_sends(d), lambda d=d: rs2_copy(j, d).start())

    def stage2(j):
        def reduce():
            for d in range(1, outer):
                rs2_copy(j, d).wait_recv()
            total = half[j, o].astype(F32)
            for d in range(1, outer):
                total += got2[j, d - 1].astype(F32)
            owner = lax.rem(y + j, n_event)
            mask = pairs_ref[pl.ds(pl.multiple_of(owner * events, 8), events), :].astype(F32)
            tile = lax.rem(o, tiles)
            chosen = mask[:, :128]
            for t in range(1, tiles):
                chosen = jnp.where(tile == t, mask[:, t * 128:(t + 1) * 128], chosen)
            chosen = jnp.concatenate([chosen, chosen], 0)
            res[j, i * per_inner + o] = (scale_one * total * chosen).astype(BF16)
            for d in range(1, outer):
                ag2_copy(j, d, o).start()

        when(o < per_inner, reduce)

    def stage3(j):
        for d in range(1, outer):
            source = lax.rem(o - d + outer, outer)
            when(source < per_inner, lambda d=d, source=source: ag2_copy(j, d, source).wait_recv())
        for d in range(1, inner):
            ag1_copy(j, d, i).start()

    def stage4(j):
        for d in range(1, inner):
            ag1_copy(j, d, lax.rem(i - d + inner, inner)).wait_recv()

    acc[...] = jnp.zeros_like(acc)

    def backward(j, k):
        def one(n, carry):
            f = k * per_part + n
            both = jnp.concatenate([res[j, f * tiles + t].astype(F32) for t in range(tiles)], 1)
            real, imag = both[:events], both[events:]
            left = jnp.concatenate(
                [jnp.concatenate([real, imag], 1), jnp.concatenate([imag, -real], 1)], 0
            ).astype(BF16)
            back = jnp.dot(left, g[f], preferred_element_type=F32)
            terms = back * s[j, f].astype(F32)
            total = terms[:8]
            for r in range(1, 2 * events // 8):
                total += terms[r * 8:(r + 1) * 8]
            acc[...] += total
            return carry

        lax.fori_loop(0, per_part, one, None)

    for k in range(inner):
        forward(0, k, True)
    for j in range(n_event):
        if j + 1 < n_event:
            beside = [functools.partial(forward, j + 1, k, False) for k in range(inner)]
            if j > 0:
                beside += [functools.partial(backward, j - 1, k) for k in range(inner)]
        else:
            beside = [functools.partial(backward, j - 1, k) for k in range(inner)] if j > 0 else []
        stages = [stage1, stage2, stage3, stage4]
        for n, stage in enumerate(stages):
            stage(j)
            if n < 3:
                cut = len(beside) * (n + 1) // 3
                for fn in beside[len(beside) * n // 3:cut]:
                    fn()
    for k in range(inner):
        backward(n_event - 1, k)

    local = acc[:, :cells]
    for c in range(1, comps):
        local += acc[:, c * cells:(c + 1) * cells]
    ends[0] = local

    def end_copy(d):
        return remote(ends.at[0], ends.at[d], end_s.at[d - 1], end_r.at[d - 1], at_event(-d))

    for d in range(1, n_event):
        end_copy(d).start()

    for j in range(1, n_event):
        for f in range(freqs):
            strain_copy(j, f).wait_send()
    for j in range(n_event):
        for d in range(1, inner):
            rs1_copy(j, d).wait_send()
            ag1_copy(j, d, i).wait_send()
        for d in range(1, outer):
            when(rs2_sends(d), lambda d=d, j=j: rs2_copy(j, d).wait_send())
            when(o < per_inner, lambda d=d, j=j: ag2_copy(j, d, o).wait_send())
    for d in range(1, n_event):
        end_copy(d).wait_recv()
    total = ends[0]
    for d in range(1, n_event):
        total += ends[d]
    total = scale_two * jnp.sum(total, axis=0, keepdims=True)
    width = cells // n_event
    mine = total[:, :width]
    for e in range(1, n_event):
        mine = jnp.where(y == e, total[:, e * width:(e + 1) * width], mine)
    out_ref[...] = mine
    for d in range(1, n_event):
        end_copy(d).wait_send()


def body(green, strain, perturb, pairs):
    freqs, recv = green.shape[0], green.shape[1]
    comps, cells = green.shape[3], green.shape[4]
    events = strain.shape[0]
    n_space = lax.axis_size("space")
    n_event = lax.axis_size("event")
    inner = 4
    outer = n_space // inner
    units = freqs * (recv // 128)
    per_inner = units // inner
    rows = 2 * comps
    flat_green = green.transpose(0, 1, 3, 2, 4).reshape(freqs, recv * rows, cells)
    flat_strain = strain.transpose(0, 1, 3, 2, 4).reshape(events * freqs * rows, cells)
    dma = pltpu.SemaphoreType.DMA
    wide = comps * cells
    hess = pl.pallas_call(
        functools.partial(kernel, n_space, n_event, inner, freqs, recv, comps, cells, events),
        out_shape=jax.ShapeDtypeStruct((1, cells // n_event), F32),
        in_specs=[
            pl.BlockSpec(memory_space=pl.ANY),
            pl.BlockSpec(memory_space=pl.ANY),
            pl.BlockSpec(memory_space=pltpu.VMEM),
            pl.BlockSpec(memory_space=pltpu.VMEM),
        ],
        out_specs=pl.BlockSpec(memory_space=pltpu.VMEM),
        scratch_shapes=[
            pltpu.VMEM((freqs, recv * rows, cells), BF16),
            pltpu.VMEM((events * freqs * rows, cells), BF16),
            pltpu.VMEM((recv * rows, cells), F32),
            pltpu.VMEM((events * freqs * rows, cells), F32),
            pltpu.VMEM((freqs, 2 * recv, wide), BF16),
            pltpu.VMEM((n_event, freqs, 2 * events, wide), BF16),
            pltpu.VMEM((n_event, units, 2 * events, 128), BF16),
            pltpu.VMEM((n_event, inner - 1, per_inner, 2 * events, 128), BF16),
            pltpu.VMEM((n_event, per_inner, 2 * events, 128), BF16),
            pltpu.VMEM((n_event, outer - 1, 2 * events, 128), BF16),
            pltpu.VMEM((n_event, units, 2 * events, 128), BF16),
            pltpu.VMEM((8, wide), F32),
            pltpu.VMEM((n_event, 8, cells), F32),
            dma((freqs + 1,)),
            dma((n_event - 1, freqs)),
            dma((n_event - 1, freqs)),
            dma((n_event, inner - 1)),
            dma((n_event, inner - 1)),
            dma((n_event, outer - 1)),
            dma((n_event, outer - 1)),
            dma((n_event, outer - 1)),
            dma((n_event, outer - 1)),
            dma((n_event, inner - 1)),
            dma((n_event, inner - 1)),
            dma((n_event - 1,)),
            dma((n_event - 1,)),
        ],
        compiler_params=pltpu.CompilerParams(
            collective_id=0, has_side_effects=True, vmem_limit_bytes=60 * 1024 * 1024
        ),
    )(flat_green, flat_strain, perturb.reshape(1, cells), pairs)
    return hess.reshape(-1)


def solution(mesh):
    in_specs = (
        P(None, "event", None, None, "space"),
        P("event", None, None, None, "space"),
        P("space"),
        P(None, "event"),
    )
    out_specs = P(("space", "event"))
    return jax.shard_map(body, mesh=mesh, in_specs=in_specs, out_specs=out_specs, check_vma=False)
```

time: 154 us -> 41.4 us (0.27)
  waiting for transfers between devices: 101 us -> 0 us
  Pallas kernels: 0 us -> 40 us
  local copies, waits for them, and re-layouts: 21.2 us -> 1.19 us
  between operations: 14.2 us -> 0.01 us
  matrix products: 6.93 us -> 0 us
  other arithmetic: 4.99 us -> 0 us
  blocking collectives: 4.94 us -> 0 us
    psum x1 -> x0, waiting for transfers between devices: 90.9 us -> none  [body(): total = lax.psum(partial_data, 'space')]
    pallas_call x0 -> x1, Pallas kernels: none -> 40 us  [body(): pl.pallas_call(functools.partial(kernel, n_space, n_event, inner, freqs,...]
    unnamed x13 -> x1, local copies, waits for them, and re-layouts: 21 us -> 1.19 us
    all_gather x1 -> x0, waiting for transfers between devices: 9.72 us -> none  [body(): everything = lax.all_gather(strain, 'event', axis=0, tiled=True)]
    dot_general x2 -> x0, matrix products: 6.93 us -> none  [the longest x1 4.89 us: body(): jnp.einsum('fqepr,frpk->fqek', back_in, flat_green, preferred_element_typ...]
    unnamed x1 -> x0, blocking collectives: 4.94 us -> none
    convert_element_type x2 -> x0, other arithmetic: 2.7 us -> none  [the longest x1 1.5 us: body(): weighted = (everything.astype(jnp.float32) * perturb).astype(jnp.bfloat16)]
  transfers between devices with their start and end apart: 2 -> 0, of which waited for: 2 -> 0; matrix products, arithmetic and copies ran while one was open for 11% -> 0% of each run, Pallas kernels for 0% -> 0%
where the time goes in v1:
time: 41.4 us; the launch traced here: 41.2 us
  Pallas kernels  40 us (97%)
  local copies, waits for them, and re-layouts  1.19 us (3%)
    pallas_call x1, Pallas kernels, body(): pl.pallas_call(functools.partial(kernel, n_space, n_event, inner, freqs,...  40 us
    unnamed x1, local copies, waits for them, and re-layouts  1.19 us

profile of v1, /device:TPU:0, one launch (start us, length us, event | category | flops | bytes accessed | tf_op | source)
XLA Modules:
  0.0 41.2 jit_solution(17322036212444870486)
XLA Ops:
  0.0 40.0 %shard_map.46 = f32[1,64]{1,0:T(1,128)} custom-call(bf16[8,3072,128]{2,1,0:T(8,128)(2,1)} %bitcast.8, bf16[2304,128]{1,0:T(8,128)(2,1)} %bitcast.9, f32[1,128]{1,0:T(1,128)} %bitcast.10, s32[48,256]{1,0:T(8,128)} %pairs_ref.1), custom_call_target="tpu_custom_call" | custom-call | tf_op jit(solution)/shard_map/pallas_call | solution.py:278
  40.0 1.2 %copy.6 = f32[64]{0:T(128)} copy(f32[64]{0:T(128)} %bitcast.11) | data formatting | bytes 512

commit v2 on v0

v2 whole, which is shorter than its diff:
```python
import functools
import math

import jax
import jax.numpy as jnp
from jax import lax
from jax.experimental import pallas as pl
from jax.experimental.pallas import tpu as pltpu
from jax.sharding import PartitionSpec as P

MESH = pl.DeviceIdType.MESH
F32 = jnp.float32
BF16 = jnp.bfloat16


def each(count, fn):
    if count <= 16:
        for n in range(count):
            fn(n)
    else:
        lax.fori_loop(0, count, lambda n, carry: (fn(n), carry)[1], None)


def kernel(
    n_space, n_event, freqs, recv, comps, cells, events,
    green_ref, strain_ref, perturb_ref, pairs_ref, out_ref,
    raw_green, raw_strain, wide_green, wide_strain, g, s, part, got, res, acc, ends,
    load_sem, strain_s, strain_r, rs_s, rs_r, ag_s, ag_r, end_s, end_r,
):
    tiles = recv // 128
    units = freqs * tiles
    rows = 2 * comps
    block = 2 * events
    ahead = min(3, freqs)
    lag = 2
    scale_one = 1.0 / math.sqrt(12.0 * cells * n_space)

    me = lax.axis_index("space")
    y = lax.axis_index("event")
    my_freq = lax.div(me, tiles)

    def at_event(d):
        return {"event": lax.rem(y + d + n_event, n_event)}

    def peer(d):
        return lax.rem(me + 1 + d, n_space)

    def remote(src, dst, send, recv_, device):
        return pltpu.make_async_remote_copy(
            src_ref=src, dst_ref=dst, send_sem=send, recv_sem=recv_, device_id=device, device_id_type=MESH
        )

    def when(cond, fn):
        if units == n_space:
            fn()
        else:
            pl.when(cond)(fn)

    strain_load = pltpu.make_async_copy(strain_ref, raw_strain, load_sem.at[freqs])
    strain_load.start()

    def green_load(f):
        return pltpu.make_async_copy(green_ref.at[f], raw_green.at[f], load_sem.at[f])

    for f in range(freqs):
        green_load(f).start()

    barrier = pltpu.get_barrier_semaphore()
    for d in range(1, n_event):
        pl.semaphore_signal(barrier, inc=1, device_id=at_event(d), device_id_type=MESH)

    def greet(d):
        pl.semaphore_signal(barrier, inc=1, device_id={"space": peer(d)}, device_id_type=MESH)

    each(n_space - 1, greet)

    strain_load.wait()
    wide_strain[...] = raw_strain[...].astype(F32)
    pl.semaphore_wait(barrier, n_event + n_space - 2)

    def strain_copy(j, f):
        return remote(s.at[0, f], s.at[j, f], strain_s.at[j - 1, f], strain_r.at[j - 1, f], at_event(-j))

    def arrange_strain(f):
        for c in range(comps):
            pieces = [
                wide_strain[pl.ds(f * rows + 2 * c + q, events, stride=freqs * rows), :] for q in range(2)
            ]
            s[0, f, :, c * cells:(c + 1) * cells] = jnp.concatenate(pieces, 0).astype(BF16)
        for j in range(1, n_event):
            strain_copy(j, f).start()

    for f in range(ahead):
        arrange_strain(f)

    perturb = jnp.concatenate([perturb_ref[...]] * comps, 1)

    def arrange_green(f):
        green_load(f).wait()
        wide_green[...] = raw_green[f].astype(F32)
        for c in range(comps):
            for p in range(2):
                g[f, p * recv:(p + 1) * recv, c * cells:(c + 1) * cells] = wide_green[
                    pl.ds(2 * c + p, recv, stride=rows), :
                ].astype(BF16)

    def rs_copy(j, unit, source):
        return remote(
            part.at[j, unit], got.at[j, source], rs_s.at[j, unit], rs_r.at[j, source], {"space": unit}
        )

    def ag_copy(j, d, unit):
        spot = res.at[j, unit]
        return remote(spot, spot, ag_s.at[j, d], ag_r.at[j, unit], {"space": peer(d)})

    def forward(j, f):
        weighted = (s[j, f].astype(F32) * perturb).astype(BF16)
        both = lax.dot_general(weighted, g[f], (((1,), (1,)), ((), ())), preferred_element_type=F32)
        real = both[:events, :recv] - both[events:, recv:]
        imag = both[events:, :recv] + both[:events, recv:]
        data = jnp.concatenate([real, imag], 0).astype(BF16)
        for t in range(tiles):
            unit = f * tiles + t
            part[j, unit] = data[:, t * 128:(t + 1) * 128]
            pl.when(me != unit)(lambda unit=unit: rs_copy(j, unit, me).start())

    def reduce(j):
        def wait(d):
            rs_copy(j, me, peer(d)).wait_recv()

        each(n_space - 1, wait)
        total = part[j, me].astype(F32)
        for d in range(n_space - 1):
            total += got[j, peer(d)].astype(F32)
        owner = lax.rem(y + j, n_event)
        mask = pairs_ref[pl.ds(pl.multiple_of(owner * events, 8), events), :].astype(F32)
        tile = lax.rem(me, tiles)
        chosen = mask[:, :128]
        for t in range(1, tiles):
            chosen = jnp.where(tile == t, mask[:, t * 128:(t + 1) * 128], chosen)
        chosen = jnp.concatenate([chosen, chosen], 0)
        res[j, me] = (scale_one * total * chosen).astype(BF16)
        each(n_space - 1, lambda d: ag_copy(j, d, me).start())

    acc[...] = jnp.zeros_like(acc)

    def backward(j, f):
        for t in range(tiles):
            unit = f * tiles + t
            pl.when(me != unit)(lambda unit=unit: ag_copy(j, 0, unit).wait_recv())
        both = jnp.concatenate([res[j, f * tiles + t].astype(F32) for t in range(tiles)], 1)
        real, imag = both[:events], both[events:]
        left = jnp.concatenate(
            [jnp.concatenate([real, imag], 1), jnp.concatenate([imag, -real], 1)], 0
        ).astype(BF16)
        back = jnp.dot(left, g[f], preferred_element_type=F32)
        terms = back * s[j, f].astype(F32)
        total = terms[:8]
        for r in range(1, block // 8):
            total += terms[r * 8:(r + 1) * 8]
        acc[...] += total

    def loop(fn):
        lax.fori_loop(0, freqs, lambda f, carry: (fn(f), carry)[1], None)

    def first(f):
        arrange_green(f)
        forward(0, f)
        pl.when(f + ahead < freqs)(lambda: arrange_strain(f + ahead))

    def reduce_at(j, step):
        when(me < units, lambda: pl.when(step == my_freq + lag)(lambda: reduce(j)))

    loop(first)
    when(me < units, lambda: reduce(0))
    for j in range(1, n_event):
        def following(f, j=j):
            for q in range(j, j + 1):
                strain_copy(q, f).wait_recv()
            forward(j, f)
            reduce_at(j, f)

        loop(following)

        def between(f, j=j):
            reduce_at(j, f + freqs)
            backward(j - 1, f)

        loop(between)
    loop(lambda f: backward(n_event - 1, f))

    local = acc[:, :cells]
    for c in range(1, comps):
        local += acc[:, c * cells:(c + 1) * cells]
    ends[0] = local

    def end_copy(d):
        return remote(ends.at[0], ends.at[d], end_s.at[d - 1], end_r.at[d - 1], at_event(-d))

    for d in range(1, n_event):
        end_copy(d).start()

    for j in range(1, n_event):
        for f in range(freqs):
            strain_copy(j, f).wait_send()
    for j in range(n_event):
        def sent(unit, j=j):
            pl.when(me != unit)(lambda: rs_copy(j, unit, me).wait_send())

        each(units, sent)
        when(me < units, lambda j=j: each(n_space - 1, lambda d: ag_copy(j, d, me).wait_send()))
    for d in range(1, n_event):
        end_copy(d).wait_recv()
    total = ends[0]
    for d in range(1, n_event):
        total += ends[d]
    total = jnp.sum(total, axis=0, keepdims=True)
    width = cells // n_event
    mine = total[:, :width]
    for e in range(1, n_event):
        mine = jnp.where(y == e, total[:, e * width:(e + 1) * width], mine)
    out_ref[...] = mine
    for d in range(1, n_event):
        end_copy(d).wait_send()


def body(green, strain, perturb, pairs):
    freqs, recv = green.shape[0], green.shape[1]
    comps, cells = green.shape[3], green.shape[4]
    events = strain.shape[0]
    n_space = lax.axis_size("space")
    n_event = lax.axis_size("event")
    units = freqs * (recv // 128)
    rows = 2 * comps
    scale_two = 1.0 / math.sqrt(12.0 * events * n_event * freqs * recv * n_event)
    flat_green = green.transpose(0, 1, 3, 2, 4).reshape(freqs, recv * rows, cells)
    flat_strain = strain.transpose(0, 1, 3, 2, 4).reshape(events * freqs * rows, cells)
    dma = pltpu.SemaphoreType.DMA
    wide = comps * cells
    hess = pl.pallas_call(
        functools.partial(kernel, n_space, n_event, freqs, recv, comps, cells, events),
        out_shape=jax.ShapeDtypeStruct((1, cells // n_event), F32),
        in_specs=[
            pl.BlockSpec(memory_space=pl.ANY),
            pl.BlockSpec(memory_space=pl.ANY),
            pl.BlockSpec(memory_space=pltpu.VMEM),
            pl.BlockSpec(memory_space=pltpu.VMEM),
        ],
        out_specs=pl.BlockSpec(memory_space=pltpu.VMEM),
        scratch_shapes=[
            pltpu.VMEM((freqs, recv * rows, cells), BF16),
            pltpu.VMEM((events * freqs * rows, cells), BF16),
            pltpu.VMEM((recv * rows, cells), F32),
            pltpu.VMEM((events * freqs * rows, cells), F32),
            pltpu.VMEM((freqs, 2 * recv, wide), BF16),
            pltpu.VMEM((n_event, freqs, 2 * events, wide), BF16),
            pltpu.VMEM((n_event, units, 2 * events, 128), BF16),
            pltpu.VMEM((n_event, n_space, 2 * events, 128), BF16),
            pltpu.VMEM((n_event, units, 2 * events, 128), BF16),
            pltpu.VMEM((8, wide), F32),
            pltpu.VMEM((n_event, 8, cells), F32),
            dma((freqs + 1,)),
            dma((n_event - 1, freqs)),
            dma((n_event - 1, freqs)),
            dma((n_event, units)),
            dma((n_event, n_space)),
            dma((n_event, n_space - 1)),
            dma((n_event, units)),
            dma((n_event - 1,)),
            dma((n_event - 1,)),
        ],
        compiler_params=pltpu.CompilerParams(
            collective_id=0, has_side_effects=True, vmem_limit_bytes=60 * 1024 * 1024
        ),
    )(flat_green, flat_strain, perturb.reshape(1, cells), pairs)
    return hess.reshape(-1) * scale_two


def solution(mesh):
    in_specs = (
        P(None, "event", None, None, "space"),
        P("event", None, None, None, "space"),
        P("space"),
        P(None, "event"),
    )
    out_specs = P(("space", "event"))
    return jax.shard_map(body, mesh=mesh, in_specs=in_specs, out_specs=out_specs, check_vma=False)
```

time: 154 us -> 49 us (0.32)
  waiting for transfers between devices: 101 us -> 0 us
  Pallas kernels: 0 us -> 47.6 us
  local copies, waits for them, and re-layouts: 21.2 us -> 0 us
  between operations: 14.2 us -> 0.01 us
  matrix products: 6.93 us -> 0 us
  blocking collectives: 4.94 us -> 0 us
  other arithmetic: 4.99 us -> 1.19 us
    psum x1 -> x0, waiting for transfers between devices: 90.9 us -> none  [body(): total = lax.psum(partial_data, 'space')]
    pallas_call x0 -> x1, Pallas kernels: none -> 47.6 us  [body(): pl.pallas_call(functools.partial(kernel, n_space, n_event, freqs, recv, c...]
    unnamed x13 -> x0, local copies, waits for them, and re-layouts: 21 us -> none
    all_gather x1 -> x0, waiting for transfers between devices: 9.72 us -> none  [body(): everything = lax.all_gather(strain, 'event', axis=0, tiled=True)]
    dot_general x2 -> x0, matrix products: 6.93 us -> none  [the longest x1 4.89 us: body(): jnp.einsum('fqepr,frpk->fqek', back_in, flat_green, preferred_element_typ...]
    unnamed x1 -> x0, blocking collectives: 4.94 us -> none
    convert_element_type x2 -> x0, other arithmetic: 2.7 us -> none  [the longest x1 1.5 us: body(): weighted = (everything.astype(jnp.float32) * perturb).astype(jnp.bfloat16)]
  transfers between devices with their start and end apart: 2 -> 0, of which waited for: 2 -> 0; matrix products, arithmetic and copies ran while one was open for 11% -> 0% of each run, Pallas kernels for 0% -> 0%
where the time goes in v2:
time: 49 us; the launch traced here: 48.8 us
  Pallas kernels  47.6 us (97%)
  other arithmetic  1.19 us (2%)
    pallas_call x1, Pallas kernels, body(): pl.pallas_call(functools.partial(kernel, n_space, n_event, freqs, recv, c...  47.6 us
    mul x1, other arithmetic, body(): return hess.reshape(-1) * scale_two  1.19 us

profile of v2, /device:TPU:0, one launch (start us, length us, event | category | flops | bytes accessed | tf_op | source)
XLA Modules:
  0.0 48.8 jit_solution(4326406098196807779)
XLA Ops:
  0.0 47.6 %shard_map.46 = f32[1,64]{1,0:T(1,128)} custom-call(bf16[8,3072,128]{2,1,0:T(8,128)(2,1)} %bitcast.9, bf16[2304,128]{1,0:T(8,128)(2,1)} %bitcast.10, f32[1,128]{1,0:T(1,128)} %bitcast.11, s32[48,256]{1,0:T(8,128)} %pairs_ref.1), custom_call_target="tpu_custom_call" | custom-call | tf_op jit(solution)/shard_map/pallas_call | solution.py:240
  47.6 1.2 %multiply_bitcast_fusion = f32[64]{0:T(128)} fusion(f32[1,64]{1,0:T(1,128)} %shard_map.46), kind=kLoop, calls=%fused_computation | loop fusion | flops 64 | bytes 512 | tf_op jit(solution)/shard_map/mul | solution.py:276

commit v3 on v1

--- a/solution.py
+++ b/solution.py
@@ -90,7 +90,8 @@
             strain_copy(j, f).start()
         return carry
 
-    lax.fori_loop(0, freqs, arrange_strain, None)
+    ahead = min(2, freqs)
+    lax.fori_loop(0, ahead, arrange_strain, None)
 
     perturb = jnp.concatenate([perturb_ref[...]] * comps, 1)
 
@@ -115,6 +116,9 @@
             data = jnp.concatenate([real, imag], 0).astype(BF16)
             for t in range(tiles):
                 part[j, f * tiles + t] = data[:, t * 128:(t + 1) * 128]
+            if arrange:
+                step = k * per_part + n + ahead
+                pl.when(step < freqs)(lambda: arrange_strain(step, None))
             return carry
 
         lax.fori_loop(0, per_part, one, None)
@@ -181,15 +185,15 @@
         for d in range(1, inner):
             ag1_copy(j, d, i).start()
 
-    def stage4(j):
-        for d in range(1, inner):
-            ag1_copy(j, d, lax.rem(i - d + inner, inner)).wait_recv()
-
     acc[...] = jnp.zeros_like(acc)
 
     def backward(j, k):
+        from_inner = lax.rem(i - k + inner, inner)
+        if k > 0:
+            ag1_copy(j, k, from_inner).wait_recv()
+
         def one(n, carry):
-            f = k * per_part + n
+            f = from_inner * per_part + n
             both = jnp.concatenate([res[j, f * tiles + t].astype(F32) for t in range(tiles)], 1)
             real, imag = both[:events], both[events:]
             left = jnp.concatenate(
@@ -214,12 +218,11 @@
                 beside += [functools.partial(backward, j - 1, k) for k in range(inner)]
         else:
             beside = [functools.partial(backward, j - 1, k) for k in range(inner)] if j > 0 else []
-        stages = [stage1, stage2, stage3, stage4]
-        for n, stage in enumerate(stages):
+        for n, stage in enumerate([stage1, stage2, stage3]):
             stage(j)
-            if n < 3:
-                cut = len(beside) * (n + 1) // 3
-                for fn in beside[len(beside) * n // 3:cut]:
+            if n < 2 or j + 1 < n_event:
+                cut = len(beside) * (n + 1) // (3 if j + 1 < n_event else 2)
+                for fn in beside[len(beside) * n // (3 if j + 1 < n_event else 2):cut]:
                     fn()
     for k in range(inner):
         backward(n_event - 1, k)

time: 41.4 us -> 39.5 us (0.954)
  Pallas kernels: 40 us -> 38.1 us
    pallas_call x1, Pallas kernels: 40 us -> 38.1 us  [body(): pl.pallas_call(functools.partial(kernel, n_space, n_event, inner, freqs,...]
where the time goes in v3:
time: 39.5 us; the launch traced here: 39.3 us
  Pallas kernels  38.1 us (96%)
  local copies, waits for them, and re-layouts  1.19 us (3%)
    pallas_call x1, Pallas kernels, body(): pl.pallas_call(functools.partial(kernel, n_space, n_event, inner, freqs,...  38.1 us
    unnamed x1, local copies, waits for them, and re-layouts  1.19 us

profile of v3, /device:TPU:0, one launch (start us, length us, event | category | flops | bytes accessed | tf_op | source)
XLA Modules:
  0.0 39.3 jit_solution(9242382970887156410)
XLA Ops:
  0.0 38.1 %shard_map.46 = f32[1,64]{1,0:T(1,128)} custom-call(bf16[8,3072,128]{2,1,0:T(8,128)(2,1)} %bitcast.8, bf16[2304,128]{1,0:T(8,128)(2,1)} %bitcast.9, f32[1,128]{1,0:T(1,128)} %bitcast.10, s32[48,256]{1,0:T(8,128)} %pairs_ref.1), custom_call_target="tpu_custom_call" | custom-call | tf_op jit(solution)/shard_map/pallas_call | solution.py:281
  38.1 1.2 %copy.6 = f32[64]{0:T(128)} copy(f32[64]{0:T(128)} %bitcast.11) | data formatting | bytes 512

commit v4 on v3

--- a/solution.py
+++ b/solution.py
@@ -86,12 +86,16 @@
                 wide_strain[pl.ds(f * rows + 2 * c + q, events, stride=freqs * rows), :] for q in range(2)
             ]
             s[0, f, :, c * cells:(c + 1) * cells] = jnp.concatenate(pieces, 0).astype(BF16)
+        return carry
+
+    def send_strain(k):
         for j in range(1, n_event):
-            strain_copy(j, f).start()
-        return carry
+            strain_copy(j, order(k)).start()
 
     ahead = min(2, freqs)
-    lax.fori_loop(0, ahead, arrange_strain, None)
+    for k in range(ahead):
+        arrange_strain(k, None)
+        send_strain(k)
 
     perturb = jnp.concatenate([perturb_ref[...]] * comps, 1)
 
@@ -109,16 +113,18 @@
             if j > 0:
                 for step in range(j, j + 1):
                     strain_copy(step, f).wait_recv()
-            weighted = (s[j, f].astype(F32) * perturb).astype(BF16)
-            both = lax.dot_general(weighted, g[f], (((1,), (1,)), ((), ())), preferred_element_type=F32)
-            real = both[:events, :recv] - both[events:, recv:]
-            imag = both[events:, :recv] + both[:events, recv:]
-            data = jnp.concatenate([real, imag], 0).astype(BF16)
+            weighted = s[j, f].astype(F32) * perturb
+            swapped = jnp.concatenate([-weighted[events:], weighted[:events]], 0)
+            along = (((1,), (1,)), ((), ()))
+            data = lax.dot_general(g[f, :recv], weighted.astype(BF16), along, preferred_element_type=F32)
+            data += lax.dot_general(g[f, recv:], swapped.astype(BF16), along, preferred_element_type=F32)
+            data = data.T.astype(BF16)
             for t in range(tiles):
                 part[j, f * tiles + t] = data[:, t * 128:(t + 1) * 128]
             if arrange:
-                step = k * per_part + n + ahead
-                pl.when(step < freqs)(lambda: arrange_strain(step, None))
+                step = k * per_part + n
+                pl.when(step + ahead < freqs)(lambda: arrange_strain(step + ahead, None))
+                pl.when(lax.rem(step, 2) == 1)(lambda: send_strain(ahead + lax.div(step, 2)))
             return carry
 
         lax.fori_loop(0, per_part, one, None)
@@ -220,6 +226,9 @@
             beside = [functools.partial(backward, j - 1, k) for k in range(inner)] if j > 0 else []
         for n, stage in enumerate([stage1, stage2, stage3]):
             stage(j)
+            if j == 0 and n < 2:
+                for k in range(ahead + freqs // 2 + n, freqs, 2):
+                    send_strain(k)
             if n < 2 or j + 1 < n_event:
                 cut = len(beside) * (n + 1) // (3 if j + 1 < n_event else 2)
                 for fn in beside[len(beside) * n // (3 if j + 1 < n_event else 2):cut]:

time: 39.5 us -> 39.8 us (level)
  no operation moved by 1% of the time
where the time goes in v4:
time: 39.8 us; the launch traced here: 39.6 us
  Pallas kernels  38.4 us (96%)
  local copies, waits for them, and re-layouts  1.19 us (3%)
    pallas_call x1, Pallas kernels, body(): pl.pallas_call(functools.partial(kernel, n_space, n_event, inner, freqs,...  38.4 us
    unnamed x1, local copies, waits for them, and re-layouts  1.19 us

profile of v4, /device:TPU:0, one launch (start us, length us, event | category | flops | bytes accessed | tf_op | source)
XLA Modules:
  0.0 39.6 jit_solution(7574248057742441726)
XLA Ops:
  0.0 38.4 %shard_map.46 = f32[1,64]{1,0:T(1,128)} custom-call(bf16[8,3072,128]{2,1,0:T(8,128)(2,1)} %bitcast.8, bf16[2304,128]{1,0:T(8,128)(2,1)} %bitcast.9, f32[1,128]{1,0:T(1,128)} %bitcast.10, s32[48,256]{1,0:T(8,128)} %pairs_ref.1), custom_call_target="tpu_custom_call" | custom-call | tf_op jit(solution)/shard_map/pallas_call | solution.py:290
  38.4 1.2 %copy.6 = f32[64]{0:T(128)} copy(f32[64]{0:T(128)} %bitcast.11) | data formatting | bytes 512

commit v5 on v4

--- a/solution.py
+++ b/solution.py
@@ -92,7 +92,7 @@
         for j in range(1, n_event):
             strain_copy(j, order(k)).start()
 
-    ahead = min(2, freqs)
+    ahead = min(3, freqs)
     for k in range(ahead):
         arrange_strain(k, None)
         send_strain(k)
@@ -123,8 +123,11 @@
                 part[j, f * tiles + t] = data[:, t * 128:(t + 1) * 128]
             if arrange:
                 step = k * per_part + n
-                pl.when(step + ahead < freqs)(lambda: arrange_strain(step + ahead, None))
-                pl.when(lax.rem(step, 2) == 1)(lambda: send_strain(ahead + lax.div(step, 2)))
+
+                @pl.when(step + ahead < freqs)
+                def _():
+                    arrange_strain(step + ahead, None)
+                    send_strain(step + ahead)
             return carry
 
         lax.fori_loop(0, per_part, one, None)
@@ -218,21 +221,27 @@
     for k in range(inner):
         forward(0, k, True)
     for j in range(n_event):
-        if j + 1 < n_event:
-            beside = [functools.partial(forward, j + 1, k, False) for k in range(inner)]
+        last = j + 1 == n_event
+        if not last:
+            forward(j + 1, 0, False)
+        stage1(j)
+        if not last:
+            forward(j + 1, 1, False)
+        elif j > 0:
+            backward(j - 1, 0)
+            backward(j - 1, 1)
+        stage2(j)
+        if not last:
+            forward(j + 1, 2, False)
+        elif j > 0:
+            backward(j - 1, 2)
+            backward(j - 1, 3)
+        stage3(j)
+        if not last:
+            forward(j + 1, 3, False)
             if j > 0:
-                beside += [functools.partial(backward, j - 1, k) for k in range(inner)]
-        else:
-            beside = [functools.partial(backward, j - 1, k) for k in range(inner)] if j > 0 else []
-        for n, stage in enumerate([stage1, stage2, stage3]):
-            stage(j)
-            if j == 0 and n < 2:
-                for k in range(ahead + freqs // 2 + n, freqs, 2):
-                    send_strain(k)
-            if n < 2 or j + 1 < n_event:
-                cut = len(beside) * (n + 1) // (3 if j + 1 < n_event else 2)
-                for fn in beside[len(beside) * n // (3 if j + 1 < n_event else 2):cut]:
-                    fn()
+                for k in range(inner):
+                    backward(j - 1, k)
     for k in range(inner):
         backward(n_event - 1, k)
 

time: 39.8 us -> 38.4 us (0.965)
  Pallas kernels: 38.4 us -> 37 us
    pallas_call x1, Pallas kernels: 38.4 us -> 37 us  [body(): pl.pallas_call(functools.partial(kernel, n_space, n_event, inner, freqs,...]
where the time goes in v5:
time: 38.4 us; the launch traced here: 38.2 us
  Pallas kernels  37 us (96%)
  local copies, waits for them, and re-layouts  1.19 us (3%)
    pallas_call x1, Pallas kernels, body(): pl.pallas_call(functools.partial(kernel, n_space, n_event, inner, freqs,...  37 us
    unnamed x1, local copies, waits for them, and re-layouts  1.19 us

profile of v5, /device:TPU:0, one launch (start us, length us, event | category | flops | bytes accessed | tf_op | source)
XLA Modules:
  0.0 38.2 jit_solution(10441048078353617001)
XLA Ops:
  0.0 37.0 %shard_map.46 = f32[1,64]{1,0:T(1,128)} custom-call(bf16[8,3072,128]{2,1,0:T(8,128)(2,1)} %bitcast.8, bf16[2304,128]{1,0:T(8,128)(2,1)} %bitcast.9, f32[1,128]{1,0:T(1,128)} %bitcast.10, s32[48,256]{1,0:T(8,128)} %pairs_ref.1), custom_call_target="tpu_custom_call" | custom-call | tf_op jit(solution)/shard_map/pallas_call | solution.py:299
  37.0 1.2 %copy.6 = f32[64]{0:T(128)} copy(f32[64]{0:T(128)} %bitcast.11) | data formatting | bytes 512

commit v6 on v5

--- a/solution.py
+++ b/solution.py
@@ -99,9 +99,9 @@
 
     perturb = jnp.concatenate([perturb_ref[...]] * comps, 1)
 
-    def forward(j, k, arrange):
-        def one(n, carry):
-            f = order(k * per_part + n)
+    def forward(j, first, count, arrange):
+        def one(step, carry):
+            f = order(step)
             if arrange:
                 green_load(f).wait()
                 wide_green[...] = raw_green[f].astype(F32)
@@ -111,8 +111,7 @@
                             pl.ds(2 * c + p, recv, stride=rows), :
                         ].astype(BF16)
             if j > 0:
-                for step in range(j, j + 1):
-                    strain_copy(step, f).wait_recv()
+                strain_copy(j, f).wait_recv()
             weighted = s[j, f].astype(F32) * perturb
             swapped = jnp.concatenate([-weighted[events:], weighted[:events]], 0)
             along = (((1,), (1,)), ((), ()))
@@ -122,17 +121,18 @@
             for t in range(tiles):
                 part[j, f * tiles + t] = data[:, t * 128:(t + 1) * 128]
             if arrange:
-                step = k * per_part + n
-
                 @pl.when(step + ahead < freqs)
                 def _():
                     arrange_strain(step + ahead, None)
                     send_strain(step + ahead)
+
+            @pl.when((lax.rem(step, per_part) == per_part - 1) & (step < freqs - per_part))
+            def _():
+                rs1_copy(j, lax.div(step, per_part) + 1).start()
+
             return carry
 
-        lax.fori_loop(0, per_part, one, None)
-        if k < inner - 1:
-            rs1_copy(j, k + 1).start()
+        lax.fori_loop(first * per_part, (first + count) * per_part, one, None)
 
     def rs1_copy(j, d):
         target = lax.rem(i + d, inner)
@@ -196,13 +196,16 @@
 
     acc[...] = jnp.zeros_like(acc)
 
-    def backward(j, k):
-        from_inner = lax.rem(i - k + inner, inner)
-        if k > 0:
-            ag1_copy(j, k, from_inner).wait_recv()
-
-        def one(n, carry):
-            f = from_inner * per_part + n
+    def backward(j, first, count):
+        def one(step, carry):
+            k = lax.div(step, per_part)
+            from_inner = lax.rem(i - k + inner, inner)
+
+            @pl.when((lax.rem(step, per_part) == 0) & (k > 0))
+            def _():
+                ag1_copy(j, k, from_inner).wait_recv()
+
+            f = from_inner * per_part + lax.rem(step, per_part)
             both = jnp.concatenate([res[j, f * tiles + t].astype(F32) for t in range(tiles)], 1)
             real, imag = both[:events], both[events:]
             left = jnp.concatenate(
@@ -216,34 +219,29 @@
             acc[...] += total
             return carry
 
-        lax.fori_loop(0, per_part, one, None)
-
-    for k in range(inner):
-        forward(0, k, True)
+        lax.fori_loop(first * per_part, (first + count) * per_part, one, None)
+
+    forward(0, 0, inner, True)
     for j in range(n_event):
         last = j + 1 == n_event
         if not last:
-            forward(j + 1, 0, False)
+            forward(j + 1, 0, 1, False)
         stage1(j)
         if not last:
-            forward(j + 1, 1, False)
+            forward(j + 1, 1, 1, False)
         elif j > 0:
-            backward(j - 1, 0)
-            backward(j - 1, 1)
+            backward(j - 1, 0, 2)
         stage2(j)
         if not last:
-            forward(j + 1, 2, False)
+            forward(j + 1, 2, 1, False)
         elif j > 0:
-            backward(j - 1, 2)
-            backward(j - 1, 3)
+            backward(j - 1, 2, 2)
         stage3(j)
         if not last:
-            forward(j + 1, 3, False)
+            forward(j + 1, 3, 1, False)
             if j > 0:
-                for k in range(inner):
-                    backward(j - 1, k)
-    for k in range(inner):
-        backward(n_event - 1, k)
+                backward(j - 1, 0, inner)
+    backward(n_event - 1, 0, inner)
 
     local = acc[:, :cells]
     for c in range(1, comps):

time: 38.4 us -> 38 us (0.990)
  Pallas kernels: 37 us -> 36.6 us
where the time goes in v6:
time: 38 us; the launch traced here: 37.9 us
  Pallas kernels  36.6 us (96%)
  local copies, waits for them, and re-layouts  1.19 us (3%)
    pallas_call x1, Pallas kernels, body(): pl.pallas_call(functools.partial(kernel, n_space, n_event, inner, freqs,...  36.6 us
    unnamed x1, local copies, waits for them, and re-layouts  1.19 us

profile of v6, /device:TPU:0, one launch (start us, length us, event | category | flops | bytes accessed | tf_op | source)
XLA Modules:
  0.0 37.9 jit_solution(15860255051567976599)
XLA Ops:
  0.0 36.6 %shard_map.46 = f32[1,64]{1,0:T(1,128)} custom-call(bf16[8,3072,128]{2,1,0:T(8,128)(2,1)} %bitcast.8, bf16[2304,128]{1,0:T(8,128)(2,1)} %bitcast.9, f32[1,128]{1,0:T(1,128)} %bitcast.10, s32[48,256]{1,0:T(8,128)} %pairs_ref.1), custom_call_target="tpu_custom_call" | custom-call | tf_op jit(solution)/shard_map/pallas_call | solution.py:297
  36.7 1.2 %copy.6 = f32[64]{0:T(128)} copy(f32[64]{0:T(128)} %bitcast.11) | data formatting | bytes 512

commit v7 on v6

--- a/solution.py
+++ b/solution.py
@@ -152,9 +152,9 @@
         spot = res.at[j, i * per_inner + t]
         return remote(spot, spot, ag2_s.at[j, d - 1], ag2_r.at[j, d - 1], at_outer(d))
 
-    def ag1_copy(j, d, which):
-        spot = res.at[j, pl.ds(which * per_inner, per_inner)]
-        return remote(spot, spot, ag1_s.at[j, d - 1], ag1_r.at[j, d - 1], at_inner(d))
+    def ag1_copy(j, d, which, t):
+        spot = res.at[j, which * per_inner + t]
+        return remote(spot, spot, ag1_s.at[j, d - 1, t], ag1_r.at[j, d - 1, t], at_inner(d))
 
     def stage1(j):
         for d in range(1, inner):
@@ -184,15 +184,21 @@
             res[j, i * per_inner + o] = (scale_one * total * chosen).astype(BF16)
             for d in range(1, outer):
                 ag2_copy(j, d, o).start()
+            for d in range(1, inner):
+                ag1_copy(j, d, i, o).start()
 
         when(o < per_inner, reduce)
 
     def stage3(j):
         for d in range(1, outer):
             source = lax.rem(o - d + outer, outer)
-            when(source < per_inner, lambda d=d, source=source: ag2_copy(j, d, source).wait_recv())
-        for d in range(1, inner):
-            ag1_copy(j, d, i).start()
+
+            def pass_on(d=d, source=source):
+                ag2_copy(j, d, source).wait_recv()
+                for e in range(1, inner):
+                    ag1_copy(j, e, i, source).start()
+
+            when(source < per_inner, pass_on)
 
     acc[...] = jnp.zeros_like(acc)
 
@@ -201,11 +207,14 @@
             k = lax.div(step, per_part)
             from_inner = lax.rem(i - k + inner, inner)
 
-            @pl.when((lax.rem(step, per_part) == 0) & (k > 0))
+            n = lax.rem(step, per_part)
+
+            @pl.when(k > 0)
             def _():
-                ag1_copy(j, k, from_inner).wait_recv()
-
-            f = from_inner * per_part + lax.rem(step, per_part)
+                for t in range(tiles):
+                    ag1_copy(j, k, from_inner, n * tiles + t).wait_recv()
+
+            f = from_inner * per_part + n
             both = jnp.concatenate([res[j, f * tiles + t].astype(F32) for t in range(tiles)], 1)
             real, imag = both[:events], both[events:]
             left = jnp.concatenate(
@@ -260,7 +269,8 @@
     for j in range(n_event):
         for d in range(1, inner):
             rs1_copy(j, d).wait_send()
-            ag1_copy(j, d, i).wait_send()
+            for t in range(per_inner):
+                ag1_copy(j, d, i, t).wait_send()
         for d in range(1, outer):
             when(rs2_sends(d), lambda d=d, j=j: rs2_copy(j, d).wait_send())
             when(o < per_inner, lambda d=d, j=j: ag2_copy(j, d, o).wait_send())
@@ -327,8 +337,8 @@
             dma((n_event, outer - 1)),
             dma((n_event, outer - 1)),
             dma((n_event, outer - 1)),
-            dma((n_event, inner - 1)),
-            dma((n_event, inner - 1)),
+            dma((n_event, inner - 1, per_inner)),
+            dma((n_event, inner - 1, per_inner)),
             dma((n_event - 1,)),
             dma((n_event - 1,)),
         ],

time: 38 us -> 38.5 us (1.013)
  Pallas kernels: 36.6 us -> 37.1 us
    pallas_call x1, Pallas kernels: 36.6 us -> 37.1 us  [body(): pl.pallas_call(functools.partial(kernel, n_space, n_event, inner, freqs,...]
where the time goes in v7:
time: 38.5 us; the launch traced here: 38.3 us
  Pallas kernels  37.1 us (96%)
  local copies, waits for them, and re-layouts  1.19 us (3%)
    pallas_call x1, Pallas kernels, body(): pl.pallas_call(functools.partial(kernel, n_space, n_event, inner, freqs,...  37.1 us
    unnamed x1, local copies, waits for them, and re-layouts  1.19 us

profile of v7, /device:TPU:0, one launch (start us, length us, event | category | flops | bytes accessed | tf_op | source)
XLA Modules:
  0.0 38.3 jit_solution(16326230773528250786)
XLA Ops:
  0.0 37.1 %shard_map.46 = f32[1,64]{1,0:T(1,128)} custom-call(bf16[8,3072,128]{2,1,0:T(8,128)(2,1)} %bitcast.8, bf16[2304,128]{1,0:T(8,128)(2,1)} %bitcast.9, f32[1,128]{1,0:T(1,128)} %bitcast.10, s32[48,256]{1,0:T(8,128)} %pairs_ref.1), custom_call_target="tpu_custom_call" | custom-call | tf_op jit(solution)/shard_map/pallas_call | solution.py:307
  37.1 1.2 %copy.6 = f32[64]{0:T(128)} copy(f32[64]{0:T(128)} %bitcast.11) | data formatting | bytes 512

commit v8 on v6

--- a/solution.py
+++ b/solution.py
@@ -197,29 +197,29 @@
     acc[...] = jnp.zeros_like(acc)
 
     def backward(j, first, count):
-        def one(step, carry):
-            k = lax.div(step, per_part)
+        def one(k, carry):
             from_inner = lax.rem(i - k + inner, inner)
 
-            @pl.when((lax.rem(step, per_part) == 0) & (k > 0))
+            @pl.when(k > 0)
             def _():
                 ag1_copy(j, k, from_inner).wait_recv()
 
-            f = from_inner * per_part + lax.rem(step, per_part)
-            both = jnp.concatenate([res[j, f * tiles + t].astype(F32) for t in range(tiles)], 1)
-            real, imag = both[:events], both[events:]
-            left = jnp.concatenate(
-                [jnp.concatenate([real, imag], 1), jnp.concatenate([imag, -real], 1)], 0
-            ).astype(BF16)
-            back = jnp.dot(left, g[f], preferred_element_type=F32)
-            terms = back * s[j, f].astype(F32)
-            total = terms[:8]
-            for r in range(1, 2 * events // 8):
-                total += terms[r * 8:(r + 1) * 8]
-            acc[...] += total
+            total = acc[...]
+            for n in range(per_part):
+                f = from_inner * per_part + n
+                both = jnp.concatenate([res[j, f * tiles + t].astype(F32) for t in range(tiles)], 1)
+                real, imag = both[:events], both[events:]
+                left = jnp.concatenate(
+                    [jnp.concatenate([real, imag], 1), jnp.concatenate([imag, -real], 1)], 0
+                ).astype(BF16)
+                back = jnp.dot(left, g[f], preferred_element_type=F32)
+                terms = back * s[j, f].astype(F32)
+                for r in range(2 * events // 8):
+                    total += terms[r * 8:(r + 1) * 8]
+            acc[...] = total
             return carry
 
-        lax.fori_loop(first * per_part, (first + count) * per_part, one, None)
+        lax.fori_loop(first, first + count, one, None)
 
     forward(0, 0, inner, True)
     for j in range(n_event):

time: 38 us -> 37.8 us (level)
  no operation moved by 1% of the time
where the time goes in v8:
time: 37.8 us; the launch traced here: 37.6 us
  Pallas kernels  36.4 us (96%)
  local copies, waits for them, and re-layouts  1.19 us (3%)
    pallas_call x1, Pallas kernels, body(): pl.pallas_call(functools.partial(kernel, n_space, n_event, inner, freqs,...  36.4 us
    unnamed x1, local copies, waits for them, and re-layouts  1.19 us

profile of v8, /device:TPU:0, one launch (start us, length us, event | category | flops | bytes accessed | tf_op | source)
XLA Modules:
  0.0 37.6 jit_solution(10320680020606086062)
XLA Ops:
  0.0 36.4 %shard_map.46 = f32[1,64]{1,0:T(1,128)} custom-call(bf16[8,3072,128]{2,1,0:T(8,128)(2,1)} %bitcast.8, bf16[2304,128]{1,0:T(8,128)(2,1)} %bitcast.9, f32[1,128]{1,0:T(1,128)} %bitcast.10, s32[48,256]{1,0:T(8,128)} %pairs_ref.1), custom_call_target="tpu_custom_call" | custom-call | tf_op jit(solution)/shard_map/pallas_call | solution.py:297
  36.4 1.2 %copy.6 = f32[64]{0:T(128)} copy(f32[64]{0:T(128)} %bitcast.11) | data formatting | bytes 512
